TPU v7x, 256 devices: a whole 4x4x8 slice. The times are simulated.
256 devices in a mesh: ctx: 64 (over z, y, core), head: 4 (over x).
Axes of the slice: x: 4, y: 4, z: 8, core: 2. Of those that a mesh axis runs over, the one named last changes fastest.
Arguments:
- queries: bfloat16 [8192, 8192], P('ctx', 'head'), may hold values from -6 to 6
- key_states: bfloat16 [8192, 1024], P('ctx', 'head'), may hold values from -6 to 6
- value_states: bfloat16 [8192, 1024], P('ctx', 'head'), may hold values from -6 to 6
- keep_pages: int32 [8, 64, 8], P('head', 'ctx'), may hold values from 0 to 7, each once within a row
- keep_count: int32 [8, 64], P('head'), may hold values from 1 to 8, as said below
- dest_slot: int32 [8, 64, 8], P('head'), may hold values from 0 to 511, as said below
Outputs:
- attention: bfloat16 [8192, 8192], P('ctx', 'head')
- key_importance: float32 [8192], P('ctx')
- page_tiles: bfloat16 [64, 8, 8, 4096], P('ctx', 'head')
- page_scale: float32 [64, 8, 8, 2], P('ctx', 'head')
- key_bounds: float32 [64, 8, 8, 2, 128], P('ctx', 'head')
- page_score: float32 [64, 8, 8], P('ctx', 'head')
Inputs may be any that keep to these rules, and one draw needn't show every extreme that they name: `keep_pages`: every list holds each page number of its block once. `keep_count`: some block of each KV head keeps all of its 8 pages. `dest_slot`: within one KV head, the entries of all blocks name distinct slots, so each owner has 8 places for each KV head. The owner of an entry of block c is (c + d) mod 64 with 0 <= d < 8; for each KV head and block, every such d is named by the same number of entries of the list, 1 of them.
All inputs are finite; a program needn't handle non-finite values. Where the computation divides by a largest or mean magnitude, that divisor is 1e-20 or more.
Results may differ from a plain program's by a relative error of at most 0.0055.
Values may be sent and summed in bfloat16 or wider, within the bound.
A program may use at most 64 MiB of HBM per device.

v0:
```python
from functools import partial
import math

import jax
import jax.numpy as jnp
from jax import lax
from jax.sharding import PartitionSpec as P

HEAD_DIM = 128
PAGE = 16


negative_fill = -1e30
quant_levels = 7.0
amax_epsilon = 1e-06


def from_behind(value, axis, by):
    size = lax.axis_size(axis)
    return lax.ppermute(value, axis, [(i, (i + by) % size) for i in range(size)])


def requantize(flat_tiles):
    entries = flat_tiles.shape[0]
    halves = flat_tiles.reshape(entries, 2, PAGE * HEAD_DIM).astype(jnp.float32)
    amax = jnp.max(jnp.abs(halves), axis=2)
    normalized = (halves * quant_levels / (amax + amax_epsilon)[..., None]).astype(jnp.bfloat16)
    key_rows = halves[:, 0].reshape(entries, PAGE, HEAD_DIM)
    bounds = jnp.stack([jnp.min(key_rows, axis=1), jnp.max(key_rows, axis=1)], axis=1)
    return (normalized.reshape(entries, 2 * PAGE * HEAD_DIM), amax / quant_levels, bounds)


def head_scores(query_heads, key_block, score_scale):
    return (
        jnp.einsum("tagd,rad->agtr", query_heads, key_block, preferred_element_type=jnp.float32)
        * score_scale
    )


def split_blocks(row_count):
    block_rows = math.gcd(row_count, 512)
    return (block_rows, row_count // block_rows)


def attend_rows(state_in, pieces, first_row, query_heads, query_pos, score_scale, skipping):
    key_piece, value_piece = pieces
    kv_local = query_heads.shape[1]
    block_rows, block_count = split_blocks(key_piece.shape[0])
    key_blocks = key_piece.reshape(block_count, block_rows, kv_local, HEAD_DIM)
    value_blocks = value_piece.reshape(block_count, block_rows, kv_local, HEAD_DIM)

    def attend_block_step(state_now, block_index):
        key_pos = block_index * block_rows + jnp.arange(block_rows, dtype=jnp.int32)
        running, row_total, weighted = state_now
        visible = key_pos[None, :] <= query_pos[:, None]
        scores = jnp.where(
            visible, head_scores(query_heads, key_blocks[block_index], score_scale), negative_fill
        )
        new_max = jnp.maximum(running, jnp.max(scores, axis=-1))
        weights = jnp.where(visible, jnp.exp(scores - new_max[..., None]), 0.0)
        factor = jnp.exp(running - new_max)
        row_total = row_total * factor + jnp.sum(weights, axis=-1)
        update = jnp.einsum(
            "agtr,rad->agtd",
            weights.astype(jnp.bfloat16),
            value_blocks[block_index],
            preferred_element_type=jnp.float32,
        )
        result = (new_max, row_total, weighted * factor[..., None] + update)
        return (result, None)

    final_state, unused = lax.scan(
        attend_block_step, state_in, jnp.arange(block_count, dtype=jnp.int32)
    )
    return final_state


def column_rows(
    sums_in, key_piece, first_row, query_heads, query_pos, log_totals, score_scale, skipping
):
    kv_local = query_heads.shape[1]
    block_rows, block_count = split_blocks(key_piece.shape[0])
    key_blocks = key_piece.reshape(block_count, block_rows, kv_local, HEAD_DIM)

    def column_block_step(sums_now, block_index):
        offset = block_index * block_rows
        key_pos = offset + jnp.arange(block_rows, dtype=jnp.int32)
        visible = key_pos[None, :] <= query_pos[:, None]
        scores = jnp.where(
            visible, head_scores(query_heads, key_blocks[block_index], score_scale), negative_fill
        )
        weights = jnp.where(visible, jnp.exp(scores - log_totals[..., None]), 0.0)
        columns = jnp.sum(weights, axis=(1, 2))
        existing = lax.dynamic_slice_in_dim(sums_now, offset, block_rows, 1)
        result = lax.dynamic_update_slice_in_dim(sums_now, existing + columns, offset, 1)
        return (result, None)

    final_sums, unused = lax.scan(
        column_block_step, sums_in, jnp.arange(block_count, dtype=jnp.int32)
    )
    return final_sums


def on_device(queries, key_states, value_states, keep_pages, keep_count, dest_slot):
    tok_rows = queries.shape[0]
    kv_local = key_states.shape[1] // HEAD_DIM
    group_size = queries.shape[1] // (kv_local * HEAD_DIM)
    devices = lax.axis_size("ctx")
    my_index = lax.axis_index("ctx")
    total_len = tok_rows * devices
    page_count = tok_rows // PAGE
    score_scale = 1.0 / math.sqrt(HEAD_DIM)
    query_pos = my_index * tok_rows + jnp.arange(tok_rows, dtype=jnp.int32)
    query_heads = queries.reshape(tok_rows, kv_local, group_size, HEAD_DIM)
    start_state = (
        jnp.full((kv_local, group_size, tok_rows), negative_fill, jnp.float32),
        jnp.zeros((kv_local, group_size, tok_rows), jnp.float32),
        jnp.zeros((kv_local, group_size, tok_rows, HEAD_DIM), jnp.float32),
    )
    attend_fold = partial(
        attend_rows,
        query_heads=query_heads,
        query_pos=query_pos,
        score_scale=score_scale,
        skipping=False,
    )
    zero_sums = jnp.zeros((kv_local, total_len), jnp.float32)
    running, row_total, weighted = attend_fold(
        start_state,
        (
            lax.all_gather(key_states, "ctx", axis=0, tiled=True),
            lax.all_gather(value_states, "ctx", axis=0, tiled=True),
        ),
        jnp.int32(0),
    )
    log_totals = running + jnp.log(row_total)
    column_fold = partial(
        column_rows,
        query_heads=query_heads,
        query_pos=query_pos,
        log_totals=log_totals,
        score_scale=score_scale,
        skipping=False,
    )
    sums = column_fold(
        zero_sums, lax.all_gather(key_states, "ctx", axis=0, tiled=True), jnp.int32(0)
    )
    mixed = weighted / row_total[..., None]
    attention = jnp.transpose(mixed, (2, 0, 1, 3)).reshape(
        tok_rows, kv_local * group_size * HEAD_DIM
    )
    attention = attention.astype(jnp.bfloat16)
    own_sums = lax.psum_scatter(sums, "ctx", scatter_dimension=1, tiled=True)
    column_score = own_sums * (total_len / group_size) / (total_len - query_pos).astype(jnp.float32)
    key_importance = lax.psum(jnp.sum(column_score, axis=0), "head")
    page_mean = column_score.reshape(kv_local, page_count, PAGE).mean(axis=-1)
    tile_width = 2 * PAGE * HEAD_DIM
    key_pages = jnp.transpose(
        key_states.reshape(page_count, PAGE, kv_local, HEAD_DIM), (2, 0, 1, 3)
    ).reshape(kv_local, page_count, PAGE * HEAD_DIM)
    value_pages = jnp.transpose(
        value_states.reshape(page_count, PAGE, kv_local, HEAD_DIM), (2, 0, 1, 3)
    ).reshape(kv_local, page_count, PAGE * HEAD_DIM)
    tiles = jnp.concatenate([key_pages, value_pages], axis=-1)
    page_ids = jnp.arange(page_count, dtype=jnp.int32)
    keep_pick = keep_pages[:, 0, :][:, :, None] == page_ids[None, None, :]
    kept_tiles = jnp.einsum(
        "hjp,hpx->hjx", keep_pick.astype(jnp.bfloat16), tiles, preferred_element_type=jnp.float32
    ).astype(jnp.bfloat16)
    kept_score = jnp.einsum(
        "hjp,hp->hj", keep_pick.astype(jnp.float32), page_mean, precision=lax.Precision.HIGHEST
    )
    entry_count = kv_local * page_count
    span = min(page_count, 8)
    per_owner = page_count // span
    cap_slots = kv_local * per_owner
    block_ids = jnp.arange(devices, dtype=jnp.int32)
    owner_src = jnp.transpose(dest_slot // page_count, (1, 0, 2)).reshape(devices, entry_count)
    place_src = jnp.transpose(dest_slot % page_count, (1, 0, 2)).reshape(devices, entry_count)
    offset_src = (owner_src - block_ids[:, None]) % devices
    valid_all = page_ids[None, None, :] < keep_count[:, :, None]
    valid_src = jnp.transpose(valid_all, (1, 0, 2)).reshape(devices, entry_count)
    entry_ids = jnp.arange(entry_count, dtype=jnp.int32)
    earlier = entry_ids[None, :] < entry_ids[:, None]
    same_owner = (
        (owner_src[:, :, None] == owner_src[:, None, :]) & valid_src[:, None, :] & earlier[None]
    )
    pair_rank = jnp.sum(same_owner.astype(jnp.int32), axis=2)
    slot_ids = jnp.arange(cap_slots, dtype=jnp.int32)
    offset_ids = jnp.arange(span, dtype=jnp.int32)
    my_offset = lax.dynamic_index_in_dim(offset_src, my_index, 0, keepdims=False)
    my_valid = lax.dynamic_index_in_dim(valid_src, my_index, 0, keepdims=False)
    my_rank = lax.dynamic_index_in_dim(pair_rank, my_index, 0, keepdims=False)
    send_pick = (
        my_valid[None, None, :]
        & (my_offset[None, None, :] == offset_ids[:, None, None])
        & (my_rank[None, None, :] == slot_ids[None, :, None])
    )
    source_ids = (my_index - offset_ids) % devices
    src_owner = jnp.take(owner_src, source_ids, axis=0)
    src_place = jnp.take(place_src, source_ids, axis=0)
    src_valid = jnp.take(valid_src, source_ids, axis=0)
    source_rank = jnp.take(pair_rank, source_ids, axis=0)
    taken = src_valid & (src_owner == my_index)
    target = (entry_ids // page_count)[None, :] * page_count + src_place
    target_pick = (target[:, :, None] == entry_ids[None, None, :]) & taken[:, :, None]
    rank_pick = source_rank[:, :, None] == slot_ids[None, None, :]
    recv_pick = jnp.einsum(
        "set,sek->tsk",
        target_pick.astype(jnp.float32),
        rank_pick.astype(jnp.float32),
        precision=lax.Precision.HIGHEST,
    ).reshape(entry_count, span * cap_slots)
    flat_kept = kept_tiles.reshape(entry_count, tile_width)
    send_score = jnp.einsum(
        "oke,e->ok",
        send_pick.astype(jnp.float32),
        kept_score.reshape(entry_count),
        precision=lax.Precision.HIGHEST,
    )
    send_tiles = jnp.einsum(
        "oke,ex->okx", send_pick.astype(jnp.bfloat16), flat_kept, preferred_element_type=jnp.float32
    ).astype(jnp.bfloat16)
    tile_pieces = [send_tiles[0]]
    for offset in range(1, span):
        tile_pieces.append(from_behind(send_tiles[offset], "ctx", offset))
    arrived = jnp.stack(tile_pieces)
    placed_tiles = jnp.einsum(
        "tu,ux->tx",
        recv_pick.astype(jnp.bfloat16),
        arrived.reshape(span * cap_slots, tile_width),
        preferred_element_type=jnp.float32,
    ).astype(jnp.bfloat16)
    score_pieces = [send_score[0]]
    for offset in range(1, span):
        score_pieces.append(from_behind(send_score[offset], "ctx", offset))
    got_score = jnp.stack(score_pieces)
    slot_tiles, slot_scales, slot_bounds = requantize(placed_tiles)
    slot_score = jnp.dot(
        recv_pick, got_score.reshape(span * cap_slots), precision=lax.Precision.HIGHEST
    )
    page_tiles = slot_tiles.reshape(1, kv_local, page_count, tile_width)
    page_scale = slot_scales.reshape(1, kv_local, page_count, 2)
    key_bounds = slot_bounds.reshape(1, kv_local, page_count, 2, HEAD_DIM)
    page_score = slot_score.reshape(1, kv_local, page_count)
    return (attention, key_importance, page_tiles, page_scale, key_bounds, page_score)


def solution(mesh):
    in_specs = (
        P("ctx", "head"),
        P("ctx", "head"),
        P("ctx", "head"),
        P("head", "ctx", None),
        P("head", None),
        P("head", None, None),
    )
    out_specs = (
        P("ctx", "head"),
        P("ctx"),
        P("ctx", "head", None, None),
        P("ctx", "head", None, None),
        P("ctx", "head", None, None, None),
        P("ctx", "head", None),
    )
    return jax.shard_map(
        on_device, mesh=mesh, in_specs=in_specs, out_specs=out_specs, check_vma=False
    )
```

profile of v0, /device:TPU:1, one launch (start us, length us, event | category | flops | bytes accessed | tf_op | source)
XLA Modules:
  0.0 654.0 jit_solution(9949622583783644640)
XLA Ops:
  13.4 2.8 collective-permute-start
  21.2 3.4 collective-permute-start.4
  29.4 3.0 collective-permute-start.6
  38.4 55.7 %all-gather.3.cloned.1.call-done = bf16[8192,256]{1,0:T(8,128)(2,1)} async-done(((bf16[128,256]{1,0:T(8,128)(2,1)}), bf16[8192,256]{1,0:T(8,128)(2,1)}) %all-gather.3.cloned.1.call-update) | async-done | bytes 4194320 | tf_op jit(solution)/shard_map/all_gather | solution.py:131
  94.0 6.9 %reshape.384 = bf16[16,512,2,128]{3,2,1,0:T(2,128)(2,1)} reshape(bf16[8192,256]{1,0:T(8,128)(2,1)} %all-gather.3.cloned.1.call-done) | data formatting | bytes 8388608 | tf_op jit(solution)/shard_map/reshape | solution.py:49
  101.0 5.1 copy.378
  106.1 67.0 %all-gather.5.cloned.1.call-done = bf16[8192,256]{1,0:T(8,128)(2,1)} async-done(((bf16[128,256]{1,0:T(8,128)(2,1)}), bf16[8192,256]{1,0:T(8,128)(2,1)}) %all-gather.5.cloned.1.call-update) | async-done | bytes 4194320 | tf_op jit(solution)/shard_map/all_gather | solution.py:132
  173.1 6.9 %reshape.385 = bf16[16,512,2,128]{3,2,1,0:T(2,128)(2,1)} reshape(bf16[8192,256]{1,0:T(8,128)(2,1)} %all-gather.5.cloned.1.call-done) | data formatting | bytes 8388608 | tf_op jit(solution)/shard_map/reshape | solution.py:50
  180.1 206.5 %while.27 = (s32[]{:T(128)}, f32[2,8,128]{2,1,0:T(8,128)S(1)}, f32[2,8,128]{2,1,0:T(8,128)S(1)}, f32[2,8,128,128]{3,2,1,0:T(8,128)S(1)}, s32[16]{0:T(128)S(1)}, ...) while((s32[]{:T(128)}, f32[2,8,128]{2,1,0:T(8,128)S(1)}, ...), condition=%wide.region_3.4_spmd.clone, body=%wide.region_0.3_spmd.clone.sunk | while | flops 551365248 | bytes 33428724 | solution.py:72
  183.1 3.6 fusion.99
  186.7 3.3 fusion.100
  196.0 3.7 fusion.99
  199.6 3.3 fusion.100
  208.9 3.7 fusion.99
  212.5 3.3 fusion.100
  221.8 3.6 fusion.99
  225.4 3.3 fusion.100
  234.7 3.6 fusion.99
  238.3 3.3 fusion.100
  247.6 3.7 fusion.99
  251.3 3.3 fusion.100
  260.5 3.7 fusion.99
  264.2 3.3 fusion.100
  273.4 3.6 fusion.99
  277.1 3.3 fusion.100
  286.3 3.6 fusion.99
  290.0 3.3 fusion.100
  299.2 3.7 fusion.99
  302.9 3.3 fusion.100
  312.1 3.7 fusion.99
  315.8 3.3 fusion.100
  325.0 3.6 fusion.99
  328.7 3.3 fusion.100
  337.9 3.6 fusion.99
  341.6 3.3 fusion.100
  350.9 3.7 fusion.99
  354.5 3.3 fusion.100
  363.8 3.7 fusion.99
  367.4 3.3 fusion.100
  376.7 3.6 fusion.99
  380.3 3.3 fusion.100
  386.6 90.0 %while.26 = (s32[]{:T(128)}, f32[2,8192]{1,0:T(2,128)S(1)}, s32[16]{0:T(128)S(1)}, bf16[16,512,2,128]{3,1,2,0:T(8,128)(2,1)}, bf16[128,2,8,128]{3,0,2,1:T(8,128)...) while((s32[]{:T(128)}, f32[2,8192]{1,0:T(2,128)S(1)}, ...), condition=%wide.region_6.7_spmd.clone, body=%wide.region_4.6_spmd.clone.sunk | while | flops 273744512 | bytes 947433 | solution.py:98
  476.6 2.6 copy.414
  480.9 134.2 %reduce-scatter.4.cloned.1.call-done = f32[128,2]{1,0:T(8,128)} async-done(((f32[8192,2]{1,0:T(8,128)}), f32[128,2]{1,0:T(8,128)}) %reduce-scatter.4.cloned.1.call-update) | async-done | bytes 1040
  616.0 8.9 %psum.7 = f32[128]{0:T(128)} all-reduce(f32[128]{0:T(128)S(1)} %get-tuple-element.499), channel_id=1, replica_groups=mesh['ctx'=64,'head'=4] {'head'}, use_global_device_ids=true, to_apply=%region_9.10 | all-reduce | flops 128 | bytes 1024 | tf_op jit(solution)/shard_map/psum | solution.py:155
  625.6 8.1 %collective-permute-start.7 = (f32[2]{0:T(128)S(1)}, f32[2]{0:T(128)S(1)}, u32[]{:S(2)}, u32[]{:S(2)}) collective-permute-start(f32[2]{0:T(128)S(1)} %get-tuple-element.519), channel_id=1, source_target_pairs={{0,4},{4,8},{8,12},{12,16},{16,20},{20,24},{24,28},{28,32},{32,36}... | collective-permute-start | bytes 32 | tf_op jit(solution)/shard_map/ppermute | solution.py:20
  637.3 4.1 collective-permute-start.11
  641.5 2.4 collective-permute-start.13
  (390 shorter events, 137.2 us)
Async XLA Ops:
  7.2 86.9 %all-gather.3.cloned.1.call-start = ((), (), s32[]{:S(2)}) async-start(), calls=%async_computation.1 | async-start | bytes 4259840 | tf_op jit(solution)/shard_map/all_gather | solution.py:131
  7.9 165.2 %all-gather.5.cloned.1.call-start = ((), (), s32[]{:S(2)}) async-start(), calls=%async_computation.2 | async-start | bytes 4259840 | tf_op jit(solution)/shard_map/all_gather | solution.py:132
  8.6 606.4 %reduce-scatter.4.cloned.1.call-start = ((), (), s32[]{:S(2)}) async-start(), calls=%async_computation.3 | async-start | bytes 4259840
  13.4 14.9 %collective-permute-start = (bf16[2,4096]{1,0:T(2,128)(2,1)S(1)}, bf16[2,4096]{1,0:T(2,128)(2,1)S(1)}, u32[]{:S(2)}, u32[]{:S(2)}) collective-permute-start(bf16[2,4096]{1,0:T(2,128)(2,1)S(1)} %bitcast.211), channel_id=1, source_target_pairs={{0,4},{4,8},{8,12},{12,16},{16,20},{20,24},{24,28},{28,32},{32,36}... | collective-permute-start | bytes 49160 | tf_op jit(solution)/shard_map/ppermute | solution.py:20
  16.2 13.1 %collective-permute-start.1 = (bf16[2,4096]{1,0:T(2,128)(2,1)S(1)}, bf16[2,4096]{1,0:T(2,128)(2,1)S(1)}, u32[]{:S(2)}, u32[]{:S(2)}) collective-permute-start(bf16[2,4096]{1,0:T(2,128)(2,1)S(1)} %bitcast.210), channel_id=1, source_target_pairs={{0,8},{4,12},{8,16},{12,20},{16,24},{20,28},{24,32},{28,36},{32,40... | collective-permute-start | bytes 49160 | tf_op jit(solution)/shard_map/ppermute | solution.py:20
  17.6 16.6 %collective-permute-start.2 = (bf16[2,4096]{1,0:T(2,128)(2,1)S(1)}, bf16[2,4096]{1,0:T(2,128)(2,1)S(1)}, u32[]{:S(2)}, u32[]{:S(2)}) collective-permute-start(bf16[2,4096]{1,0:T(2,128)(2,1)S(1)} %bitcast.204), channel_id=1, source_target_pairs={{0,12},{4,16},{8,20},{12,24},{16,28},{20,32},{24,36},{28,40},{32,4... | collective-permute-start | bytes 49160 | tf_op jit(solution)/shard_map/ppermute | solution.py:20
  19.3 14.9 %collective-permute-start.3 = (bf16[2,4096]{1,0:T(2,128)(2,1)S(1)}, bf16[2,4096]{1,0:T(2,128)(2,1)S(1)}, u32[]{:S(2)}, u32[]{:S(2)}) collective-permute-start(bf16[2,4096]{1,0:T(2,128)(2,1)S(1)} %bitcast.206), channel_id=1, source_target_pairs={{0,16},{4,20},{8,24},{12,28},{16,32},{20,36},{24,40},{28,44},{32,4... | collective-permute-start | bytes 49160 | tf_op jit(solution)/shard_map/ppermute | solution.py:20
  21.2 13.1 %collective-permute-start.4 = (bf16[2,4096]{1,0:T(2,128)(2,1)S(1)}, bf16[2,4096]{1,0:T(2,128)(2,1)S(1)}, u32[]{:S(2)}, u32[]{:S(2)}) collective-permute-start(bf16[2,4096]{1,0:T(2,128)(2,1)S(1)} %bitcast.208), channel_id=1, source_target_pairs={{0,20},{4,24},{8,28},{12,32},{16,36},{20,40},{24,44},{28,48},{32,5... | collective-permute-start | bytes 49160 | tf_op jit(solution)/shard_map/ppermute | solution.py:20
  28.4 6.0 collective-permute-start.5
  29.4 5.4 collective-permute-start.6
  186.7 4.5 copy-start
  199.6 4.5 copy-start
  212.5 4.5 copy-start
  225.4 4.5 copy-start
  238.3 4.5 copy-start
  251.2 4.5 copy-start
  264.2 4.5 copy-start
  277.1 4.5 copy-start
  290.0 4.5 copy-start
  302.9 4.5 copy-start
  315.8 4.5 copy-start
  328.7 4.5 copy-start
  341.6 4.5 copy-start
  354.5 4.5 copy-start
  367.4 4.5 copy-start
  380.3 4.5 copy-start
  479.2 145.8 %copy-start.1 = (s32[2,1,8]{2,1,0:T(1,128)S(1)}, s32[2,1,8]{2,1,0:T(1,128)}, u32[]{:S(2)}) copy-start(s32[2,1,8]{2,1,0:T(1,128)} %param.15) | copy-start | bytes 196
  625.6 15.9 %collective-permute-start.7 = (f32[2]{0:T(128)S(1)}, f32[2]{0:T(128)S(1)}, u32[]{:S(2)}, u32[]{:S(2)}) collective-permute-start(f32[2]{0:T(128)S(1)} %get-tuple-element.519), channel_id=1, source_target_pairs={{0,4},{4,8},{8,12},{12,16},{16,20},{20,24},{24,28},{28,32},{32,36}... | collective-permute-start | bytes 32 | tf_op jit(solution)/shard_map/ppermute | solution.py:20
  633.7 7.8 %collective-permute-start.8 = (f32[2]{0:T(128)S(1)}, f32[2]{0:T(128)S(1)}, u32[]{:S(2)}, u32[]{:S(2)}) collective-permute-start(f32[2]{0:T(128)S(1)} %get-tuple-element.518), channel_id=1, source_target_pairs={{0,8},{4,12},{8,16},{12,20},{16,24},{20,28},{24,32},{28,36},{32,40... | collective-permute-start | bytes 32 | tf_op jit(solution)/shard_map/ppermute | solution.py:20
  634.8 9.1 %collective-permute-start.9 = (f32[2]{0:T(128)S(1)}, f32[2]{0:T(128)S(1)}, u32[]{:S(2)}, u32[]{:S(2)}) collective-permute-start(f32[2]{0:T(128)S(1)} %get-tuple-element.517), channel_id=1, source_target_pairs={{0,12},{4,16},{8,20},{12,24},{16,28},{20,32},{24,36},{28,40},{32,4... | collective-permute-start | bytes 32 | tf_op jit(solution)/shard_map/ppermute | solution.py:20
  636.5 7.4 %collective-permute-start.10 = (f32[2]{0:T(128)S(1)}, f32[2]{0:T(128)S(1)}, u32[]{:S(2)}, u32[]{:S(2)}) collective-permute-start(f32[2]{0:T(128)S(1)} %get-tuple-element.516), channel_id=1, source_target_pairs={{0,16},{4,20},{8,24},{12,28},{16,32},{20,36},{24,40},{28,44},{32,4... | collective-permute-start | bytes 32 | tf_op jit(solution)/shard_map/ppermute | solution.py:20
  637.3 6.6 %collective-permute-start.11 = (f32[2]{0:T(128)S(1)}, f32[2]{0:T(128)S(1)}, u32[]{:S(2)}, u32[]{:S(2)}) collective-permute-start(f32[2]{0:T(128)S(1)} %get-tuple-element.515), channel_id=1, source_target_pairs={{0,20},{4,24},{8,28},{12,32},{16,36},{20,40},{24,44},{28,48},{32,5... | collective-permute-start | bytes 32 | tf_op jit(solution)/shard_map/ppermute | solution.py:20
  641.5 4.5 collective-permute-start.12
  641.5 5.2 collective-permute-start.13
Sparse Core Ops, SparseCore 0:
  10.8 83.2 all-gather.2
  96.8 76.2 all-gather.4
  479.4 135.6 reduce-scatter.3
where the time goes:
time: 657 us; the launch traced here: 654 us
  waiting for transfers between devices  261 us (40%)
  matrix products  125 us (19%)
  loops' own time  80 us (12%)
  local copies, waits for them, and re-layouts  69.7 us (11%)
  other arithmetic  61.9 us (9%)
  starting transfers between devices  33.4 us (5%)
  between operations  14.1 us (2%)
  blocking collectives  8.92 us (1%)
    unnamed x4, waiting for transfers between devices  136 us
    dot_general x32, matrix products, head_scores(): jnp.einsum('tagd,rad->agtr', query_heads, key_block, preferred_element_ty...  94.7 us
    all_gather x1, waiting for transfers between devices, on_device(): lax.all_gather(value_states, 'ctx', axis=0, tiled=True)  67 us
    all_gather x1, waiting for transfers between devices, on_device(): lax.all_gather(key_states, 'ctx', axis=0, tiled=True)  55.7 us
    reduce_sum x16, other arithmetic, attend_block_step(): row_total = row_total * factor + jnp.sum(weights, axis=-1)  53.2 us
    another operation x1, loops' own time, column_rows(): lax.scan(column_block_step, sums_in, jnp.arange(block_count, dtype=jnp.in...  42.3 us
    another operation x1, loops' own time, attend_rows(): lax.scan(attend_block_step, state_in, jnp.arange(block_count, dtype=jnp.i...  37.7 us
    ppermute x14, starting transfers between devices, from_behind(): lax.ppermute(value, axis, [(i, (i + by) % size) for i in range(size)])  33.3 us
  transfers between devices with their start and end apart: 17, of which 6 were waited for; matrix products, arithmetic and copies ran while one was open for 4% of the time, Pallas kernels for 0%

commit v1 on v0

v1 whole, which is shorter than its diff:
```python
import functools

import jax
import jax.numpy as jnp
from jax import lax
from jax.experimental import pallas as pl
from jax.experimental.pallas import tpu as pltpu
from jax.sharding import PartitionSpec as P

MESH = pl.DeviceIdType.MESH
F32 = jnp.float32
BF16 = jnp.bfloat16
NZ, NY, NC, NX = 8, 4, 2, 4
NCTX = NZ * NY * NC
BLK = 128
SLAB = NY * NC * BLK
ROWS = 2 * 8 * BLK
SPAN = 8
SCALE2 = 1.4426950408889634 / 128.0**0.5
LANES = SLAB // 128


def picks_kernel(pages_ref, count_ref, slot_ref, w_ref, r_ref):
    me = lax.axis_index("ctx")
    w_ref[...] = jnp.zeros_like(w_ref)
    r_ref[...] = jnp.zeros_like(r_ref)
    one = jnp.ones((1, 128), F32)

    def entry(e, carry):
        h = e // 8
        j = e % 8
        slot = slot_ref[h, me, j]
        off = lax.rem(slot // 8 - me + NCTX, NCTX)

        @pl.when(j < count_ref[h, me])
        def _():
            w_ref[pl.ds((off * 2 + h) * 8 + pages_ref[h, 0, j], 1), :] = one

        return carry

    lax.fori_loop(0, 16, entry, 0)

    def source(e, carry):
        d = e // 16
        h = (e // 8) % 2
        j = e % 8
        src = lax.rem(me - d + NCTX, NCTX)
        slot = slot_ref[h, src, j]

        @pl.when((j < count_ref[h, src]) & (slot // 8 == me))
        def _():
            r_ref[pl.ds((d * 2 + h) * 8 + lax.rem(slot, 8), 1), :] = one

        return carry

    lax.fori_loop(0, 128, source, 0)


def qk(a, b):
    return lax.dot_general(a, b, (((1,), (1,)), ((), ())), preferred_element_type=F32)


def main_kernel(
    q_ref, k_ref, v_ref, w_ref, r_ref,
    att_ref, imp_ref, tile_ref, scale_ref, bound_ref, score_ref,
    qb, kvb, prob, mx, run_m, run_l, acc, osend, csum, csr, tot8, t2, impb, impr, tsend, trecv,
    ssend, srecv, loc_sem, sib_s, sib_r, ya_s, ya_r, yb_s, yb_r, ra_s, ra_r, rb_s, rb_r,
    pg_s, pg_r, c1_s, c1_r, c2_s, c2_r, im_s, im_r, sc_s, sc_r, o_s, o_r,
):
    me = lax.axis_index("ctx")
    hx = lax.axis_index("head")
    z = me // 8
    y = lax.rem(me // 2, 4)
    a = lax.rem(me, 2)
    b = 1 - a
    me8 = lax.rem(me, 8)

    def at(zz, yy, cc):
        return (zz * 8 + yy * 2 + cc, hx)

    def zoff(d):
        return at(lax.rem(z + d + NZ, NZ), y, a)

    def yoff(d):
        return at(z, lax.rem(y + d, NY), a)

    def slaboff(d):
        return (z * 8 + lax.rem(me8 + d, 8), hx)

    def ctxoff(d):
        return (lax.rem(me + d + NCTX, NCTX), hx)

    sib = at(z, y, b)

    def remote(src, dst, ss, rs, dev):
        return pltpu.make_async_remote_copy(
            src_ref=src, dst_ref=dst, send_sem=ss, recv_sem=rs, device_id=dev, device_id_type=MESH
        )

    bar = pltpu.get_barrier_semaphore()
    peers = [zoff(d) for d in range(1, 8)] + [slaboff(d) for d in range(1, 8)]
    peers += [(me, lax.rem(hx + d, NX)) for d in range(1, NX)]
    peers += [ctxoff(d) for d in range(1, SPAN)] + [ctxoff(-d) for d in range(1, SPAN)]
    for dev in peers:
        pl.semaphore_signal(bar, inc=1, device_id=dev, device_id_type=MESH)
    pl.semaphore_wait(bar, len(peers))

    kv_in = (k_ref, v_ref)

    def cols(g):
        return pl.ds(pl.multiple_of(g * 128, 128), 128)

    local = []
    sib_kv = []
    ya = []
    for i in range(2):
        own = kv_in[i].at[:, cols(a)]
        local.append(pltpu.make_async_copy(own, kvb.at[i, z, y, a], loc_sem.at[i]))
        sib_kv.append(
            remote(kv_in[i].at[:, cols(b)], kvb.at[i, z, y, a], sib_s.at[i], sib_r.at[i], sib)
        )
        for d in range(1, NY):
            ya.append(
                remote(own, kvb.at[i, z, y, a], ya_s.at[i, d], ya_r.at[i, d], yoff(d))
            )
    sib_q = []
    for g in range(8):
        local.append(
            pltpu.make_async_copy(q_ref.at[:, cols(a * 8 + g)], qb.at[1, g], loc_sem.at[2 + g])
        )
        sib_q.append(
            remote(q_ref.at[:, cols(b * 8 + g)], qb.at[0, g], sib_s.at[2 + g], sib_r.at[2 + g], sib)
        )
    for c in sib_kv + ya + sib_q + local:
        c.start()

    def ring_a(i, p, sign):
        zz = lax.rem(z - sign * (p - 1) + 2 * NZ, NZ)
        blk = kvb.at[i, zz, :, a]
        k = 0 if sign > 0 else 1
        return remote(blk, blk, ra_s.at[i, k, p], ra_r.at[i, k, p], zoff(sign))

    def ring_b(i, p, sign):
        zz = lax.rem(z - sign * (p - 1) + 2 * NZ, NZ)
        blk = kvb.at[i, zz, y, b]
        k = 0 if sign > 0 else 1
        return remote(blk, blk, rb_s.at[i, k, p], rb_r.at[i, k, p], zoff(sign))

    def y_b(i, p, sign, d):
        zz = lax.rem(z - sign * p + 2 * NZ, NZ)
        blk = kvb.at[i, zz, y, b]
        k = 0 if sign > 0 else 1
        return remote(blk, blk, yb_s.at[i, k, p, d], yb_r.at[i, k, p, d], yoff(d))

    for i in range(2):
        sib_kv[i].wait_recv()
        ring_b(i, 1, 1).start()
        ring_b(i, 1, -1).start()
        for d in range(1, NY):
            y_b(i, 0, 1, d).start()

    for c in local:
        c.wait()
    for i in range(2):
        for d in range(1, NY):
            ya[i * 3 + d - 1].wait_recv()
        ring_a(i, 1, 1).start()
        ring_a(i, 1, -1).start()

    for d in range(SPAN):
        for h in range(2):
            kt = jnp.zeros((16, 128), F32)
            vt = jnp.zeros((16, 128), F32)
            for p in range(8):
                r = (d * 2 + h) * 8 + p
                w = w_ref[r : r + 1, :]
                kt += w * k_ref[p * 16 : (p + 1) * 16, h * 128 : (h + 1) * 128].astype(F32)
                vt += w * v_ref[p * 16 : (p + 1) * 16, h * 128 : (h + 1) * 128].astype(F32)
            tsend[d, h, 0:16, :] = kt.astype(BF16)
            tsend[d, h, 16:32, :] = vt.astype(BF16)
    pages = [None]
    for d in range(1, SPAN):
        pages.append(remote(tsend.at[d], trecv.at[d], pg_s.at[d], pg_r.at[d], ctxoff(d)))
        pages[d].start()

    for c in sib_q:
        c.wait_recv()
    run_m[...] = jnp.full_like(run_m, -1e30)
    run_l[...] = jnp.zeros_like(run_l)

    def fold(zz, masked):
        keys = kvb.at[0, zz]

        def tile(hc, carry):
            r = pl.ds(pl.multiple_of(hc * 1024, 1024), 1024)
            s = qk(
                qb[hc].reshape(1024, 128), keys[...].reshape(SLAB, 128)
            ) * SCALE2
            parts = [s[:, t * 128 : (t + 1) * 128] for t in range(LANES)]
            if masked:
                owner = lax.rem(a + 1 - hc + 2, 2)
                row = lax.broadcasted_iota(jnp.int32, (1024, 128), 0) % 128
                lane = lax.broadcasted_iota(jnp.int32, (1024, 128), 1)
                lim = row - lane + (y * 256 + owner * 128)
                parts = [jnp.where(lim >= t * 128, x, -1e30) for t, x in enumerate(parts)]
            m = run_m[r, :]
            top = functools.reduce(jnp.maximum, parts)
            mn = jnp.maximum(m, jnp.max(top, axis=1, keepdims=True))
            total = jnp.zeros((1024, 128), F32)
            for t in range(LANES):
                e = jnp.exp2(parts[t] - mn)
                total = total + e
                prob[zz, r, t * 128 : (t + 1) * 128] = e.astype(BF16)
            run_l[r, :] = run_l[r, :] * jnp.exp2(m - mn) + total
            run_m[r, :] = mn
            mx[zz, r, :] = mn
            return carry

        lax.fori_loop(0, 2, tile, 0)

    def phase(p, carry):
        @pl.when((p >= 1) & (p <= 4))
        def _():
            for i in range(2):
                ring_b(i, p, 1).wait_recv()

                @pl.when(p < 4)
                def _():
                    ring_b(i, p + 1, 1).start()
                    ring_b(i, p, -1).wait_recv()

                @pl.when(p < 3)
                def _():
                    ring_b(i, p + 1, -1).start()

                for d in range(1, NY):
                    y_b(i, p, 1, d).start()

                @pl.when(p < 4)
                def _():
                    for d in range(1, NY):
                        y_b(i, p, -1, d).start()

                ring_a(i, p, 1).wait_recv()

                @pl.when(p < 4)
                def _():
                    ring_a(i, p + 1, 1).start()
                    ring_a(i, p, -1).wait_recv()

                @pl.when(p < 3)
                def _():
                    ring_a(i, p + 1, -1).start()

        @pl.when(p >= 1)
        def _():
            pp = p - 1
            for i in range(2):
                for d in range(1, NY):
                    y_b(i, pp, 1, d).wait_recv()

                @pl.when((pp >= 1) & (pp < 4))
                def _():
                    for d in range(1, NY):
                        y_b(i, pp, -1, d).wait_recv()

            @pl.when(pp == 0)
            def _():
                fold(z, True)

            def side(j, c):
                up = j == 0
                zz = jnp.where(up, z - pp, z + pp - NZ)
                ok = (pp >= 1) & (zz >= 0) & (up | (pp < 4))

                @pl.when(ok)
                def _():
                    fold(zz, False)

                return c

            lax.fori_loop(0, 2, side, 0)

        return carry

    lax.fori_loop(0, 6, phase, 0)

    def finish(i, carry):
        r = pl.ds(pl.multiple_of(i * 256, 256), 256)
        lse = run_m[r, :] + jnp.log2(jnp.sum(run_l[r, :], axis=1, keepdims=True))

        def one(zz, c):
            mx[zz, r, :] = jnp.exp2(mx[zz, r, :] - lse)
            return c

        return lax.fori_loop(0, z + 1, one, carry)

    lax.fori_loop(0, ROWS // 256, finish, 0)

    csum[...] = jnp.zeros_like(csum)

    def colpass(zz, carry):
        def rows(i, c):
            r = pl.ds(pl.multiple_of(i * 256, 256), 256)
            w = mx[zz, r, :]
            out = []
            for t in range(LANES):
                x = prob[zz, r, t * 128 : (t + 1) * 128].astype(F32) * w
                out.append(c[t] + jnp.sum(x.reshape(32, 8, 128), axis=0))
            return tuple(out)

        c = lax.fori_loop(
            0, ROWS // 256, rows, tuple(jnp.zeros((8, 128), F32) for _ in range(LANES))
        )
        for t in range(LANES):
            csum[zz, t : t + 1, :] = jnp.sum(c[t], axis=0, keepdims=True)
        return carry

    lax.fori_loop(0, z + 1, colpass, 0)

    c1 = [None]
    for d in range(1, NZ):
        zz = lax.rem(z - d + NZ, NZ)
        c1.append(remote(csum.at[zz], csr.at[d], c1_s.at[d], c1_r.at[d], zoff(-d)))
        c1[d].start()

    def weigh(hc):
        r = slice(hc * 1024, (hc + 1) * 1024)
        acc[...] = jnp.zeros_like(acc)

        def one(zz, c):
            vals = kvb.at[1, zz][...].reshape(SLAB, 128)
            acc[...] += mx[zz, r, :] * jnp.dot(prob[zz, r, :], vals, preferred_element_type=F32)
            return c

        lax.fori_loop(0, z + 1, one, 0)

    weigh(0)
    outs = []
    for g in range(8):
        osend[g] = acc[g * 128 : (g + 1) * 128, :].astype(BF16)
        outs.append(
            remote(osend.at[g], att_ref.at[:, cols(a * 8 + g)], o_s.at[g], o_r.at[g], sib)
        )
        outs[g].start()

    total = csum[z]
    for d in range(1, NZ):
        c1[d].wait_recv()
        total = total + csr[d]
    for t in range(8):
        tot8[t] = jnp.broadcast_to(total[t : t + 1, :], (8, 128))
    c2 = [None]
    for d in range(1, 8):
        c2.append(
            remote(tot8.at[lax.rem(me8 + d, 8)], t2.at[d], c2_s.at[d], c2_r.at[d], slaboff(d))
        )
        c2[d].start()

    weigh(1)
    for g in range(8):
        att_ref[:, cols(a * 8 + g)] = acc[g * 128 : (g + 1) * 128, :].astype(BF16)

    same = tot8[me8]
    other = jnp.zeros((8, 128), F32)
    for d in range(1, 8):
        c2[d].wait_recv()
        if d % 2 == 0:
            same = same + t2[d]
        else:
            other = other + t2[d]
    lane = lax.broadcasted_iota(jnp.int32, (8, 128), 1)
    sub = lax.broadcasted_iota(jnp.int32, (8, 128), 0)
    pos = me * BLK + lane
    factor = (NCTX * BLK / 8.0) / (NCTX * BLK - pos).astype(F32)
    col = [jnp.where(a == 0, same, other) * factor, jnp.where(a == 0, other, same) * factor]
    impb[...] = col[0] + col[1]
    im = [None]
    for d in range(1, NX):
        im.append(
            remote(impb, impr.at[d], im_s.at[d], im_r.at[d], (me, lax.rem(hx + d, NX)))
        )
        im[d].start()
    means = [
        jnp.sum(jnp.where(lane // 16 == sub, c, 0.0), axis=1, keepdims=True) / 16.0 for c in col
    ]
    for d in range(SPAN):
        for h in range(2):
            r = (d * 2 + h) * 8
            ssend[d, h : h + 1, :] = jnp.sum(w_ref[r : r + 8, :] * means[h], axis=0, keepdims=True)
    sc = [None]
    for d in range(1, SPAN):
        sc.append(remote(ssend.at[d], srecv.at[d], sc_s.at[d], sc_r.at[d], ctxoff(d)))
        sc[d].start()

    for d in range(1, SPAN):
        pages[d].wait_recv()
    for h in range(2):
        for slot in range(8):
            kt = jnp.zeros((16, 128), F32)
            vt = jnp.zeros((16, 128), F32)
            for d in range(SPAN):
                r = (d * 2 + h) * 8 + slot
                w = r_ref[r : r + 1, :]
                src = tsend if d == 0 else trecv
                kt += w * src[d, h, 0:16, :].astype(F32)
                vt += w * src[d, h, 16:32, :].astype(F32)
            for n, x in enumerate((kt, vt)):
                amax = jnp.max(jnp.max(jnp.abs(x), axis=0, keepdims=True), axis=1, keepdims=True)
                tile_ref[h, slot, n * 16 : (n + 1) * 16, :] = (x * 7.0 / (amax + 1e-6)).astype(BF16)
                scale_ref[h, slot, n : n + 1, :] = jnp.broadcast_to(amax / 7.0, (1, 128))
            bound_ref[h, slot, 0:1, :] = jnp.min(kt, axis=0, keepdims=True)
            bound_ref[h, slot, 1:2, :] = jnp.max(kt, axis=0, keepdims=True)

    for d in range(1, SPAN):
        sc[d].wait_recv()
    for h in range(2):
        got = jnp.zeros((8, 128), F32)
        for d in range(SPAN):
            r = (d * 2 + h) * 8
            src = ssend if d == 0 else srecv
            got += r_ref[r : r + 8, :] * src[d, h : h + 1, :]
        score_ref[h] = got
    imp = impb[...]
    for d in range(1, NX):
        im[d].wait_recv()
        imp = imp + impr[d]
    imp_ref[...] = imp

    for g in range(8):
        outs[g].wait()
    for c in sib_kv + ya + sib_q:
        c.wait_send()
    for i in range(2):
        for d in range(1, NY):
            y_b(i, 0, 1, d).wait_send()
        for p in range(1, 5):
            signs = (1, -1) if p < 4 else (1,)
            for s in signs:
                ring_a(i, p, s).wait_send()
                ring_b(i, p, s).wait_send()
                for d in range(1, NY):
                    y_b(i, p, s, d).wait_send()
    for group in (pages, c1, c2, im, sc):
        for c in group[1:]:
            c.wait_send()


def on_device(queries, key_states, value_states, keep_pages, keep_count, dest_slot):
    vmem = pl.BlockSpec(memory_space=pltpu.VMEM)
    smem = pl.BlockSpec(memory_space=pltpu.SMEM)
    table = jax.ShapeDtypeStruct((128, 128), F32)
    picks = pl.pallas_call(
        picks_kernel,
        out_shape=[table, table],
        in_specs=[smem] * 3,
        out_specs=[vmem] * 2,
    )
    w, r = picks(keep_pages, keep_count, dest_slot)
    dma = pltpu.SemaphoreType.DMA
    call = pl.pallas_call(
        main_kernel,
        out_shape=[
            jax.ShapeDtypeStruct((BLK, 2048), BF16),
            jax.ShapeDtypeStruct((8, 128), F32),
            jax.ShapeDtypeStruct((2, 8, 32, 128), BF16),
            jax.ShapeDtypeStruct((2, 8, 2, 128), F32),
            jax.ShapeDtypeStruct((2, 8, 2, 128), F32),
            jax.ShapeDtypeStruct((2, 8, 128), F32),
        ],
        in_specs=[vmem] * 5,
        out_specs=[vmem] * 6,
        scratch_shapes=[
            pltpu.VMEM((2, 8, BLK, 128), BF16),
            pltpu.VMEM((2, NZ, NY, NC, BLK, 128), BF16),
            pltpu.VMEM((NZ, ROWS, SLAB), BF16),
            pltpu.VMEM((NZ, ROWS, 128), F32),
            pltpu.VMEM((ROWS, 128), F32),
            pltpu.VMEM((ROWS, 128), F32),
            pltpu.VMEM((ROWS // 2, 128), F32),
            pltpu.VMEM((8, BLK, 128), BF16),
            pltpu.VMEM((NZ, 8, 128), F32),
            pltpu.VMEM((NZ, 8, 128), F32),
            pltpu.VMEM((8, 8, 128), F32),
            pltpu.VMEM((8, 8, 128), F32),
            pltpu.VMEM((8, 128), F32),
            pltpu.VMEM((NX, 8, 128), F32),
            pltpu.VMEM((SPAN, 2, 32, 128), BF16),
            pltpu.VMEM((SPAN, 2, 32, 128), BF16),
            pltpu.VMEM((SPAN, 8, 128), F32),
            pltpu.VMEM((SPAN, 8, 128), F32),
            dma((10,)),
            dma((10,)), dma((10,)),
            dma((2, NY)), dma((2, NY)),
            dma((2, 2, 5, NY)), dma((2, 2, 5, NY)),
            dma((2, 2, 5)), dma((2, 2, 5)),
            dma((2, 2, 5)), dma((2, 2, 5)),
            dma((SPAN,)), dma((SPAN,)),
            dma((NZ,)), dma((NZ,)),
            dma((8,)), dma((8,)),
            dma((NX,)), dma((NX,)),
            dma((SPAN,)), dma((SPAN,)),
            dma((8,)), dma((8,)),
        ],
        compiler_params=pltpu.CompilerParams(
            collective_id=0, has_side_effects=True, vmem_limit_bytes=62 * 2**20
        ),
    )
    att, imp, tiles, scale, bound, score = call(queries, key_states, value_states, w, r)
    return (
        att,
        imp[0],
        tiles.reshape(1, 2, 8, 4096),
        scale[None, :, :, :, 0],
        bound[None],
        score[None, :, :, 0],
    )


def solution(mesh):
    in_specs = (
        P("ctx", "head"),
        P("ctx", "head"),
        P("ctx", "head"),
        P("head", "ctx", None),
        P("head", None),
        P("head", None, None),
    )
    out_specs = (
        P("ctx", "head"),
        P("ctx"),
        P("ctx", "head", None, None),
        P("ctx", "head", None, None),
        P("ctx", "head", None, None, None),
        P("ctx", "head", None),
    )
    return jax.shard_map(
        on_device, mesh=mesh, in_specs=in_specs, out_specs=out_specs, check_vma=False
    )
```

time: 657 us -> 103 us (0.16)
  waiting for transfers between devices: 261 us -> 0 us
  matrix products: 125 us -> 0 us
  Pallas kernels: 0 us -> 92.8 us
  loops' own time: 80 us -> 0 us
  other arithmetic: 61.9 us -> 0 us
  local copies, waits for them, and re-layouts: 69.7 us -> 8.76 us
  starting transfers between devices: 33.4 us -> 0 us
  between operations: 14.1 us -> 0.65 us
  blocking collectives: 8.92 us -> 0 us
    unnamed x4 -> x0, waiting for transfers between devices: 136 us -> none
    dot_general x54 -> x0, matrix products: 125 us -> none  [the longest x32 94.7 us: head_scores(): jnp.einsum('tagd,rad->agtr', query_heads, key_block, preferred_element_ty...]
    all_gather x2 -> x0, waiting for transfers between devices: 123 us -> none  [the longest x1 67 us: on_device(): lax.all_gather(value_states, 'ctx', axis=0, tiled=True)]
    pallas_call x0 -> x2, Pallas kernels: none -> 92.8 us  [the longest x1 85.3 us: on_device(): call(queries, key_states, value_states, w, r)]
    another operation x2 -> x0, loops' own time: 80 us -> none  [the longest x1 42.3 us: column_rows(): lax.scan(column_block_step, sums_in, jnp.arange(block_count, dtype=jnp.in...]
    reduce_sum x19 -> x0, other arithmetic: 53.4 us -> none  [the longest x16 53.2 us: attend_block_step(): row_total = row_total * factor + jnp.sum(weights, axis=-1)]
    dynamic_slice x50 -> x0, local copies, waits for them, and re-layouts: 36.9 us -> none  [the longest x32 18.4 us: attend_rows(): lax.scan(attend_block_step, state_in, jnp.arange(block_count, dtype=jnp.i...]
    ppermute x14 -> x0, starting transfers between devices: 33.3 us -> none  [from_behind(): lax.ppermute(value, axis, [(i, (i + by) % size) for i in range(size)])]
  transfers between devices with their start and end apart: 17 -> 0, of which waited for: 6 -> 0; matrix products, arithmetic and copies ran while one was open for 4% -> 0% of each run, Pallas kernels for 0% -> 0%
where the time goes in v1:
time: 103 us; the launch traced here: 102 us
  Pallas kernels  92.8 us (90%)
  local copies, waits for them, and re-layouts  8.76 us (9%)
    pallas_call x1, Pallas kernels, on_device(): call(queries, key_states, value_states, w, r)  85.3 us
    pallas_call x1, Pallas kernels, on_device(): w, r = picks(keep_pages, keep_count, dest_slot)  7.47 us
    unnamed x7, local copies, waits for them, and re-layouts  3.93 us

profile of v1, /device:TPU:1, one launch (start us, length us, event | category | flops | bytes accessed | tf_op | source)
XLA Modules:
  0.0 102.2 jit_solution(4702356030003709009)
XLA Ops:
  0.6 1.4 %copy.14.slot_ref = s32[2,64,8]{2,1,0:T(8,128)} copy(s32[2,64,8]{1,2,0:T(8,128)} %param.11) | data formatting | bytes 8192 | tf_op args[5]
  2.1 7.5 %shard_map.109 = (f32[128,128]{1,0:T(8,128)}, f32[128,128]{1,0:T(8,128)}) custom-call(s32[2,1,8]{2,1,0:T(1,128)} %pages_ref.1, s32[2,64]{1,0:T(2,128)} %count_ref.1, s32[2,64,8]{2,1,0:T(8,128)} %copy.14.slot_ref), custom_call_target="tpu_custom_call" | custom-call | tf_op jit(solution)/shard_map/pallas_call | solution.py:459
  9.5 85.3 %shard_map.110 = (bf16[128,2048]{1,0:T(8,128)(2,1)}, f32[8,128]{1,0:T(8,128)}, bf16[2,8,32,128]{3,2,1,0:T(8,128)(2,1)}, f32[2,8,2,128]{3,2,1,0:T(2,128)}, f32[2,...) custom-call(bf16[128,2048]{1,0:T(8,128)(2,1)} %q_ref.1, bf16[128,256]{1,0:T(8,128)(2,1)} %k_ref.1, bf16[128,256]{1,0:T(8,128)(2,1)} %v_ref.1, ...), custom_call_target="tpu_custom_call" | custom-call | tf_op jit(solution)/shard_map/pallas_call | solution.py:509
  94.8 0.0 copy-start
  94.8 1.2 %slice_bitcast_fusion = f32[128]{0:T(128)} fusion(f32[8,128]{1,0:T(8,128)} %get-tuple-element.17), kind=kLoop, calls=%fused_computation.1 | loop fusion | bytes 1024 | tf_op jit(solution)/shard_map/squeeze | solution.py:512
  96.0 1.3 %slice_reduce_fusion = f32[2,8]{1,0:T(2,128)} fusion(f32[2,8,128]{2,1,0:T(8,128)} %get-tuple-element.21), kind=kLoop, calls=%fused_computation | loop fusion | bytes 128 | tf_op jit(solution)/shard_map/slice | solution.py:516
  97.4 0.0 copy-done
  97.4 0.7 copy.15
  98.1 1.6 %reshape.15 = bf16[1,2,8,4096]{3,2,1,0:T(8,128)(2,1)} reshape(bf16[2,8,32,128]{3,2,1,0:T(8,128)(2,1)} %get-tuple-element.18) | data formatting | bytes 262144 | tf_op jit(solution)/shard_map/reshape | solution.py:513
  99.7 0.0 copy-start.1
  99.7 1.9 %copy.18 = bf16[128,2048]{1,0:T(8,128)(2,1)} copy(bf16[128,2048]{1,0:T(8,128)(2,1)} %get-tuple-element.28) | data formatting | bytes 1048576
  101.6 0.0 copy-done.1
  101.6 0.6 copy.19
Async XLA Ops:
  94.8 2.5 %copy-start = (f32[2,8,2,128]{3,2,1,0:T(2,128)S(1)}, f32[2,8,2,128]{3,2,1,0:T(2,128)}, u32[]{:S(2)}) copy-start(f32[2,8,2,128]{3,2,1,0:T(2,128)} %get-tuple-element.19) | copy-start | bytes 49156
  99.7 1.9 %copy-start.1 = (f32[2,8,2,128]{3,2,1,0:T(2,128)S(1)}, f32[2,8,2,128]{3,2,1,0:T(2,128)}, u32[]{:S(2)}) copy-start(f32[2,8,2,128]{3,2,1,0:T(2,128)} %get-tuple-element.20) | copy-start | bytes 49156

commit v2 on v1

--- a/solution.py
+++ b/solution.py
@@ -20,50 +20,14 @@
 LANES = SLAB // 128
 
 
-def picks_kernel(pages_ref, count_ref, slot_ref, w_ref, r_ref):
-    me = lax.axis_index("ctx")
-    w_ref[...] = jnp.zeros_like(w_ref)
-    r_ref[...] = jnp.zeros_like(r_ref)
-    one = jnp.ones((1, 128), F32)
-
-    def entry(e, carry):
-        h = e // 8
-        j = e % 8
-        slot = slot_ref[h, me, j]
-        off = lax.rem(slot // 8 - me + NCTX, NCTX)
-
-        @pl.when(j < count_ref[h, me])
-        def _():
-            w_ref[pl.ds((off * 2 + h) * 8 + pages_ref[h, 0, j], 1), :] = one
-
-        return carry
-
-    lax.fori_loop(0, 16, entry, 0)
-
-    def source(e, carry):
-        d = e // 16
-        h = (e // 8) % 2
-        j = e % 8
-        src = lax.rem(me - d + NCTX, NCTX)
-        slot = slot_ref[h, src, j]
-
-        @pl.when((j < count_ref[h, src]) & (slot // 8 == me))
-        def _():
-            r_ref[pl.ds((d * 2 + h) * 8 + lax.rem(slot, 8), 1), :] = one
-
-        return carry
-
-    lax.fori_loop(0, 128, source, 0)
-
-
 def qk(a, b):
     return lax.dot_general(a, b, (((1,), (1,)), ((), ())), preferred_element_type=F32)
 
 
 def main_kernel(
-    q_ref, k_ref, v_ref, w_ref, r_ref,
+    q_ref, k_ref, v_ref, pages_ref, count_ref, slot_ref,
     att_ref, imp_ref, tile_ref, scale_ref, bound_ref, score_ref,
-    qb, kvb, prob, mx, run_m, run_l, acc, osend, csum, csr, tot8, t2, impb, impr, tsend, trecv,
+    w_ref, r_ref, qb, kvb, prob, mx, run_m, run_l, acc, osend, csum, csr, tot8, t2, impb, impr, tsend, trecv,
     ssend, srecv, loc_sem, sib_s, sib_r, ya_s, ya_r, yb_s, yb_r, ra_s, ra_r, rb_s, rb_r,
     pg_s, pg_r, c1_s, c1_r, c2_s, c2_r, im_s, im_r, sc_s, sc_r, o_s, o_r,
 ):
@@ -131,7 +95,7 @@
         sib_q.append(
             remote(q_ref.at[:, cols(b * 8 + g)], qb.at[0, g], sib_s.at[2 + g], sib_r.at[2 + g], sib)
         )
-    for c in sib_kv + ya + sib_q + local:
+    for c in [sib_kv[0]] + ya[:3] + sib_q + [sib_kv[1]] + local:
         c.start()
 
     def ring_a(i, p, sign):
@@ -152,20 +116,56 @@
         k = 0 if sign > 0 else 1
         return remote(blk, blk, yb_s.at[i, k, p, d], yb_r.at[i, k, p, d], yoff(d))
 
-    for i in range(2):
+    def begin_b(i):
         sib_kv[i].wait_recv()
         ring_b(i, 1, 1).start()
         ring_b(i, 1, -1).start()
         for d in range(1, NY):
             y_b(i, 0, 1, d).start()
 
-    for c in local:
-        c.wait()
-    for i in range(2):
+    def begin_a(i):
         for d in range(1, NY):
             ya[i * 3 + d - 1].wait_recv()
         ring_a(i, 1, 1).start()
         ring_a(i, 1, -1).start()
+
+    begin_b(0)
+    for c in local:
+        c.wait()
+    begin_a(0)
+
+    sub8 = lax.broadcasted_iota(jnp.int32, (8, 8), 0)
+    lane8 = lax.broadcasted_iota(jnp.int32, (8, 8), 1)
+    lane64 = lax.broadcasted_iota(jnp.int32, (1, 64), 1)
+    lane864 = lax.broadcasted_iota(jnp.int32, (8, 64), 1)
+
+    def kept(h, src):
+        row = jnp.where(lane64 == src, count_ref[h : h + 1, :].astype(F32), 0.0)
+        return lane8.astype(F32) < jnp.sum(row, axis=1, keepdims=True)
+
+    def spread(hit):
+        return jnp.broadcast_to(
+            jnp.sum(jnp.where(hit, 1.0, 0.0), axis=1, keepdims=True), (8, 128)
+        )
+
+    def slot_row(h, src):
+        col = jnp.sum(
+            jnp.where(lane864 == src, slot_ref[h].astype(F32), 0.0), axis=1, keepdims=True
+        )
+        row = jnp.sum(jnp.where(sub8 == lane8, col, 0.0), axis=0, keepdims=True)
+        return row.astype(jnp.int32)
+
+    for h in range(2):
+        slots = slot_row(h, me)
+        off = ((slots >> 3) - me) & (NCTX - 1)
+        base = (pages_ref[h, 0:1, :] == sub8) & kept(h, me)
+        for d in range(SPAN):
+            r = (d * 2 + h) * 8
+            w_ref[r : r + 8, :] = spread(base & (off == d))
+            src = lax.rem(me - d + NCTX, NCTX)
+            slots = slot_row(h, src)
+            hit = ((slots >> 3) == me) & ((slots & 7) == sub8) & kept(h, src)
+            r_ref[r : r + 8, :] = spread(hit)
 
     for d in range(SPAN):
         for h in range(2):
@@ -191,22 +191,24 @@
     def fold(zz, masked):
         keys = kvb.at[0, zz]
 
-        def tile(hc, carry):
-            r = pl.ds(pl.multiple_of(hc * 1024, 1024), 1024)
+        def tile(n, carry):
+            hc = n // 2
+            r = pl.ds(n * 512, 512)
             s = qk(
-                qb[hc].reshape(1024, 128), keys[...].reshape(SLAB, 128)
+                qb[hc, (n % 2) * 4 : (n % 2) * 4 + 4].reshape(512, 128),
+                keys[...].reshape(SLAB, 128),
             ) * SCALE2
             parts = [s[:, t * 128 : (t + 1) * 128] for t in range(LANES)]
             if masked:
                 owner = lax.rem(a + 1 - hc + 2, 2)
-                row = lax.broadcasted_iota(jnp.int32, (1024, 128), 0) % 128
-                lane = lax.broadcasted_iota(jnp.int32, (1024, 128), 1)
+                row = lax.broadcasted_iota(jnp.int32, (512, 128), 0) % 128
+                lane = lax.broadcasted_iota(jnp.int32, (512, 128), 1)
                 lim = row - lane + (y * 256 + owner * 128)
                 parts = [jnp.where(lim >= t * 128, x, -1e30) for t, x in enumerate(parts)]
             m = run_m[r, :]
             top = functools.reduce(jnp.maximum, parts)
             mn = jnp.maximum(m, jnp.max(top, axis=1, keepdims=True))
-            total = jnp.zeros((1024, 128), F32)
+            total = jnp.zeros((512, 128), F32)
             for t in range(LANES):
                 e = jnp.exp2(parts[t] - mn)
                 total = total + e
@@ -216,54 +218,69 @@
             mx[zz, r, :] = mn
             return carry
 
-        lax.fori_loop(0, 2, tile, 0)
+        for n in range(4):
+            tile(n, 0)
+
+    def hop(i, p):
+        p = jnp.int32(p)
+        ring_b(i, p, 1).wait_recv()
+
+        @pl.when(p < 4)
+        def _():
+            ring_b(i, p + 1, 1).start()
+            ring_b(i, p, -1).wait_recv()
+
+        @pl.when(p < 3)
+        def _():
+            ring_b(i, p + 1, -1).start()
+
+        for d in range(1, NY):
+            y_b(i, p, 1, d).start()
+
+        @pl.when(p < 4)
+        def _():
+            for d in range(1, NY):
+                y_b(i, p, -1, d).start()
+
+        ring_a(i, p, 1).wait_recv()
+
+        @pl.when(p < 4)
+        def _():
+            ring_a(i, p + 1, 1).start()
+            ring_a(i, p, -1).wait_recv()
+
+        @pl.when(p < 3)
+        def _():
+            ring_a(i, p + 1, -1).start()
+
+    def landed(i, p):
+        for d in range(1, NY):
+            y_b(i, p, 1, d).wait_recv()
+
+        @pl.when((p >= 1) & (p < 4))
+        def _():
+            for d in range(1, NY):
+                y_b(i, p, -1, d).wait_recv()
 
     def phase(p, carry):
-        @pl.when((p >= 1) & (p <= 4))
-        def _():
-            for i in range(2):
-                ring_b(i, p, 1).wait_recv()
-
-                @pl.when(p < 4)
-                def _():
-                    ring_b(i, p + 1, 1).start()
-                    ring_b(i, p, -1).wait_recv()
-
-                @pl.when(p < 3)
-                def _():
-                    ring_b(i, p + 1, -1).start()
-
-                for d in range(1, NY):
-                    y_b(i, p, 1, d).start()
-
-                @pl.when(p < 4)
-                def _():
-                    for d in range(1, NY):
-                        y_b(i, p, -1, d).start()
-
-                ring_a(i, p, 1).wait_recv()
-
-                @pl.when(p < 4)
-                def _():
-                    ring_a(i, p + 1, 1).start()
-                    ring_a(i, p, -1).wait_recv()
-
-                @pl.when(p < 3)
-                def _():
-                    ring_a(i, p + 1, -1).start()
-
-        @pl.when(p >= 1)
-        def _():
-            pp = p - 1
-            for i in range(2):
-                for d in range(1, NY):
-                    y_b(i, pp, 1, d).wait_recv()
-
-                @pl.when((pp >= 1) & (pp < 4))
-                def _():
-                    for d in range(1, NY):
-                        y_b(i, pp, -1, d).wait_recv()
-
+        @pl.when(p <= 4)
+        def _():
+            hop(0, p)
+
+        @pl.when(p == 1)
+        def _():
+            for c in ya[3:]:
+                c.start()
+
+        @pl.when(p == 2)
+        def _():
+            begin_b(1)
+            begin_a(1)
+
+        pp = p - 1
+        landed(0, pp)
+
+        if True:
             @pl.when(pp == 0)
             def _():
                 fold(z, True)
@@ -281,28 +298,22 @@
 
             lax.fori_loop(0, 2, side, 0)
 
+        @pl.when(p >= 3)
+        def _():
+            hop(1, p - 2)
+
         return carry
 
-    lax.fori_loop(0, 6, phase, 0)
-
-    def finish(i, carry):
-        r = pl.ds(pl.multiple_of(i * 256, 256), 256)
-        lse = run_m[r, :] + jnp.log2(jnp.sum(run_l[r, :], axis=1, keepdims=True))
-
-        def one(zz, c):
-            mx[zz, r, :] = jnp.exp2(mx[zz, r, :] - lse)
-            return c
-
-        return lax.fori_loop(0, z + 1, one, carry)
-
-    lax.fori_loop(0, ROWS // 256, finish, 0)
-
+    lax.fori_loop(1, 6, phase, 0)
+
+    run_m[...] = run_m[...] + jnp.log2(jnp.sum(run_l[...], axis=1, keepdims=True))
     csum[...] = jnp.zeros_like(csum)
 
     def colpass(zz, carry):
         def rows(i, c):
             r = pl.ds(pl.multiple_of(i * 256, 256), 256)
-            w = mx[zz, r, :]
+            w = jnp.exp2(mx[zz, r, :] - run_m[r, :])
+            mx[zz, r, :] = w
             out = []
             for t in range(LANES):
                 x = prob[zz, r, t * 128 : (t + 1) * 128].astype(F32) * w
@@ -316,13 +327,18 @@
             csum[zz, t : t + 1, :] = jnp.sum(c[t], axis=0, keepdims=True)
         return carry
 
-    lax.fori_loop(0, z + 1, colpass, 0)
+    half = (z + 1) // 2
+    lax.fori_loop(0, half, colpass, 0)
+    hop(1, 4)
+    lax.fori_loop(half, z + 1, colpass, 0)
 
     c1 = [None]
     for d in range(1, NZ):
         zz = lax.rem(z - d + NZ, NZ)
         c1.append(remote(csum.at[zz], csr.at[d], c1_s.at[d], c1_r.at[d], zoff(-d)))
         c1[d].start()
+
+    lax.fori_loop(0, 5, lambda p, c: (landed(1, p), c)[1], 0)
 
     def weigh(hc):
         r = slice(hc * 1024, (hc + 1) * 1024)
@@ -396,21 +412,33 @@
     for d in range(1, SPAN):
         pages[d].wait_recv()
     for h in range(2):
-        for slot in range(8):
-            kt = jnp.zeros((16, 128), F32)
-            vt = jnp.zeros((16, 128), F32)
-            for d in range(SPAN):
-                r = (d * 2 + h) * 8 + slot
-                w = r_ref[r : r + 1, :]
-                src = tsend if d == 0 else trecv
-                kt += w * src[d, h, 0:16, :].astype(F32)
-                vt += w * src[d, h, 16:32, :].astype(F32)
-            for n, x in enumerate((kt, vt)):
-                amax = jnp.max(jnp.max(jnp.abs(x), axis=0, keepdims=True), axis=1, keepdims=True)
-                tile_ref[h, slot, n * 16 : (n + 1) * 16, :] = (x * 7.0 / (amax + 1e-6)).astype(BF16)
-                scale_ref[h, slot, n : n + 1, :] = jnp.broadcast_to(amax / 7.0, (1, 128))
-            bound_ref[h, slot, 0:1, :] = jnp.min(kt, axis=0, keepdims=True)
-            bound_ref[h, slot, 1:2, :] = jnp.max(kt, axis=0, keepdims=True)
+        got = [
+            (tsend if d == 0 else trecv)[d, h].astype(F32) for d in range(SPAN)
+        ]
+        place = [r_ref[(d * 2 + h) * 8 : (d * 2 + h) * 8 + 8, :] for d in range(SPAN)]
+        scales = []
+        for n in range(2):
+            rows = [
+                functools.reduce(
+                    jnp.add, [place[d] * got[d][t : t + 1, :] for d in range(SPAN)]
+                )
+                for t in range(n * 16, n * 16 + 16)
+            ]
+            big = functools.reduce(jnp.maximum, [jnp.abs(x) for x in rows])
+            amax = jnp.max(big, axis=1, keepdims=True)
+            scales.append(amax / 7.0)
+            for t, x in enumerate(rows):
+                c = (n * 16 + t) * 128
+                tile_ref[0, h, :, c : c + 128] = (x * 7.0 / (amax + 1e-6)).astype(BF16)
+            if n == 0:
+                low = functools.reduce(jnp.minimum, rows)
+                high = functools.reduce(jnp.maximum, rows)
+                for slot in range(8):
+                    bound_ref[0, h, slot, 0:1, :] = low[slot : slot + 1, :]
+                    bound_ref[0, h, slot, 1:2, :] = high[slot : slot + 1, :]
+        for n in range(2):
+            row = jnp.sum(jnp.where(lane == sub, scales[n], 0.0), axis=0, keepdims=True)
+            scale_ref[0, h, n : n + 1, :] = row[:, 0:8]
 
     for d in range(1, SPAN):
         sc[d].wait_recv()
@@ -420,12 +448,13 @@
             r = (d * 2 + h) * 8
             src = ssend if d == 0 else srecv
             got += r_ref[r : r + 8, :] * src[d, h : h + 1, :]
-        score_ref[h] = got
+        row = jnp.sum(jnp.where(lane == sub, got, 0.0), axis=0, keepdims=True)
+        score_ref[0, h : h + 1, :] = row[:, 0:8]
     imp = impb[...]
     for d in range(1, NX):
         im[d].wait_recv()
         imp = imp + impr[d]
-    imp_ref[...] = imp
+    imp_ref[...] = imp[0:1, :]
 
     for g in range(8):
         outs[g].wait()
@@ -446,31 +475,29 @@
             c.wait_send()
 
 
+def hand_over_kernel(*refs):
+    for i in range(6):
+        refs[6 + i][...] = refs[i][...]
+
+
 def on_device(queries, key_states, value_states, keep_pages, keep_count, dest_slot):
     vmem = pl.BlockSpec(memory_space=pltpu.VMEM)
-    smem = pl.BlockSpec(memory_space=pltpu.SMEM)
-    table = jax.ShapeDtypeStruct((128, 128), F32)
-    picks = pl.pallas_call(
-        picks_kernel,
-        out_shape=[table, table],
-        in_specs=[smem] * 3,
-        out_specs=[vmem] * 2,
-    )
-    w, r = picks(keep_pages, keep_count, dest_slot)
     dma = pltpu.SemaphoreType.DMA
     call = pl.pallas_call(
         main_kernel,
         out_shape=[
             jax.ShapeDtypeStruct((BLK, 2048), BF16),
-            jax.ShapeDtypeStruct((8, 128), F32),
-            jax.ShapeDtypeStruct((2, 8, 32, 128), BF16),
-            jax.ShapeDtypeStruct((2, 8, 2, 128), F32),
-            jax.ShapeDtypeStruct((2, 8, 2, 128), F32),
-            jax.ShapeDtypeStruct((2, 8, 128), F32),
+            jax.ShapeDtypeStruct((1, 128), F32),
+            jax.ShapeDtypeStruct((1, 2, 8, 4096), BF16),
+            jax.ShapeDtypeStruct((1, 2, 2, 8), F32),
+            jax.ShapeDtypeStruct((1, 2, 8, 2, 128), F32),
+            jax.ShapeDtypeStruct((1, 2, 8), F32),
         ],
-        in_specs=[vmem] * 5,
+        in_specs=[vmem] * 6,
         out_specs=[vmem] * 6,
         scratch_shapes=[
+            pltpu.VMEM((128, 128), F32),
+            pltpu.VMEM((128, 128), F32),
             pltpu.VMEM((2, 8, BLK, 128), BF16),
             pltpu.VMEM((2, NZ, NY, NC, BLK, 128), BF16),
             pltpu.VMEM((NZ, ROWS, SLAB), BF16),
@@ -506,15 +533,16 @@
             collective_id=0, has_side_effects=True, vmem_limit_bytes=62 * 2**20
         ),
     )
-    att, imp, tiles, scale, bound, score = call(queries, key_states, value_states, w, r)
-    return (
-        att,
-        imp[0],
-        tiles.reshape(1, 2, 8, 4096),
-        scale[None, :, :, :, 0],
-        bound[None],
-        score[None, :, :, 0],
+    slots = jnp.transpose(dest_slot, (0, 2, 1))
+    made = call(queries, key_states, value_states, keep_pages, keep_count, slots)
+    hand_over = pl.pallas_call(
+        hand_over_kernel,
+        out_shape=[jax.ShapeDtypeStruct(x.shape, x.dtype) for x in made],
+        in_specs=[vmem] * 6,
+        out_specs=[vmem] * 6,
     )
+    att, imp, tiles, scale, bound, score = hand_over(*made)
+    return (att, imp[0], tiles, jnp.transpose(scale, (0, 1, 3, 2)), bound, score)
 
 
 def solution(mesh):

time: 103 us -> 77.9 us (0.76)
  Pallas kernels: 92.8 us -> 77.1 us
  local copies, waits for them, and re-layouts: 8.76 us -> 0 us
    pallas_call x2, Pallas kernels: 92.8 us -> 77.1 us  [the longest x1 75.1 us: on_device(): call(queries, key_states, value_states, keep_pages, keep_count, slots)]
    unnamed x7 -> x0, local copies, waits for them, and re-layouts: 3.93 us -> none
    slice x2 -> x0, local copies, waits for them, and re-layouts: 2.02 us -> none  [the longest x1 1.34 us: on_device(): score[None, :, :, 0]]
    reshape x1 -> x0, local copies, waits for them, and re-layouts: 1.62 us -> none  [on_device(): tiles.reshape(1, 2, 8, 4096)]
    squeeze x1 -> x0, local copies, waits for them, and re-layouts: 1.19 us -> none  [on_device(): imp[0]]
where the time goes in v2:
time: 77.9 us; the launch traced here: 77.7 us
  Pallas kernels  77.1 us (99%)
    pallas_call x1, Pallas kernels, on_device(): call(queries, key_states, value_states, keep_pages, keep_count, slots)  75.1 us
    pallas_call x1, Pallas kernels, on_device(): att, imp, tiles, scale, bound, score = hand_over(*made)  1.95 us

profile of v2, /device:TPU:1, one launch (start us, length us, event | category | flops | bytes accessed | tf_op | source)
XLA Modules:
  0.0 77.7 jit_solution(12672102097339588030)
XLA Ops:
  0.6 75.1 %shard_map.109 = (bf16[128,2048]{1,0:T(8,128)(2,1)}, f32[1,128]{1,0:T(1,128)}, bf16[1,2,8,4096]{3,2,1,0:T(8,128)(2,1)}, f32[1,2,2,8]{3,2,1,0:T(2,128)}, f32[1,2,...) custom-call(bf16[128,2048]{1,0:T(8,128)(2,1)} %q_ref.1, bf16[128,256]{1,0:T(8,128)(2,1)} %k_ref.1, bf16[128,256]{1,0:T(8,128)(2,1)} %v_ref.1, ...), custom_call_target="tpu_custom_call" | custom-call | tf_op jit(solution)/shard_map/pallas_call | solution.py:537
  75.8 1.9 %shard_map.110 = (bf16[128,2048]{1,0:T(8,128)(2,1)}, f32[1,128]{1,0:T(1,128)}, bf16[1,2,8,4096]{3,2,1,0:T(8,128)(2,1)}, f32[1,2,2,8]{3,2,1,0:T(2,128)}, f32[1,2,...) custom-call(bf16[128,2048]{1,0:T(8,128)(2,1)} %get-tuple-element.18.refs_0_, f32[1,128]{1,0:T(1,128)} %get-tuple-element.19.refs_1_, ...), custom_call_target="tpu_custom_call" | custom-call | tf_op jit(solution)/shard_map/pallas_call | solution.py:544

commit v3 on v2

--- a/solution.py
+++ b/solution.py
@@ -27,7 +27,7 @@
 def main_kernel(
     q_ref, k_ref, v_ref, pages_ref, count_ref, slot_ref,
     att_ref, imp_ref, tile_ref, scale_ref, bound_ref, score_ref,
-    w_ref, r_ref, qb, kvb, prob, mx, run_m, run_l, acc, osend, csum, csr, tot8, t2, impb, impr, tsend, trecv,
+    w_ref, r_ref, qb, q2, kvb, prob, mx, run_m, run_l, acc, osend, csum, csr, tot8, t2, impb, impr, tsend, trecv,
     ssend, srecv, loc_sem, sib_s, sib_r, ya_s, ya_r, yb_s, yb_r, ra_s, ra_r, rb_s, rb_r,
     pg_s, pg_r, c1_s, c1_r, c2_s, c2_r, im_s, im_r, sc_s, sc_r, o_s, o_r,
 ):
@@ -95,14 +95,14 @@
         sib_q.append(
             remote(q_ref.at[:, cols(b * 8 + g)], qb.at[0, g], sib_s.at[2 + g], sib_r.at[2 + g], sib)
         )
-    for c in [sib_kv[0]] + ya[:3] + sib_q + [sib_kv[1]] + local:
+    for c in [sib_kv[0]] + local + ya[:3] + sib_q + [sib_kv[1]]:
         c.start()
 
-    def ring_a(i, p, sign):
+    def ring_a(i, p, sign, e):
         zz = lax.rem(z - sign * (p - 1) + 2 * NZ, NZ)
-        blk = kvb.at[i, zz, :, a]
+        blk = kvb.at[i, zz, lax.rem(y + e, NY), a]
         k = 0 if sign > 0 else 1
-        return remote(blk, blk, ra_s.at[i, k, p], ra_r.at[i, k, p], zoff(sign))
+        return remote(blk, blk, ra_s.at[i, k, p, e], ra_r.at[i, k, p, e], zoff(sign))
 
     def ring_b(i, p, sign):
         zz = lax.rem(z - sign * (p - 1) + 2 * NZ, NZ)
@@ -123,14 +123,20 @@
         for d in range(1, NY):
             y_b(i, 0, 1, d).start()
 
+    def begin_own(i):
+        local[i].wait()
+        ring_a(i, 1, 1, 0).start()
+        ring_a(i, 1, -1, 0).start()
+
     def begin_a(i):
         for d in range(1, NY):
-            ya[i * 3 + d - 1].wait_recv()
-        ring_a(i, 1, 1).start()
-        ring_a(i, 1, -1).start()
-
+            ya[i * 3 + NY - d - 1].wait_recv()
+            ring_a(i, 1, 1, d).start()
+            ring_a(i, 1, -1, d).start()
+
+    begin_own(0)
     begin_b(0)
-    for c in local:
+    for c in local[2:]:
         c.wait()
     begin_a(0)
 
@@ -188,19 +194,29 @@
     run_m[...] = jnp.full_like(run_m, -1e30)
     run_l[...] = jnp.zeros_like(run_l)
 
+    def split(n, carry):
+        hc = n // 8
+        g = lax.rem(n, 8)
+        x = qb[hc, g].astype(F32) * SCALE2
+        hi = x.astype(BF16)
+        q2[pl.ds(pl.multiple_of(n * 128, 128), 128), 0:128] = hi
+        q2[pl.ds(pl.multiple_of(n * 128, 128), 128), 128:256] = (x - hi.astype(F32)).astype(BF16)
+        return carry
+
+    lax.fori_loop(0, 16, split, 0)
+
     def fold(zz, masked):
-        keys = kvb.at[0, zz]
-
-        def tile(n, carry):
-            hc = n // 2
-            r = pl.ds(n * 512, 512)
-            s = qk(
-                qb[hc, (n % 2) * 4 : (n % 2) * 4 + 4].reshape(512, 128),
-                keys[...].reshape(SLAB, 128),
-            ) * SCALE2
+        block = kvb.at[0, zz][...].reshape(SLAB, 128)
+        keys = jnp.concatenate([block, block], axis=1)
+
+        def logits(n):
+            return qk(q2[n * 512 : (n + 1) * 512, :], keys)
+
+        def absorb(n, s):
+            r = slice(n * 512, (n + 1) * 512)
             parts = [s[:, t * 128 : (t + 1) * 128] for t in range(LANES)]
             if masked:
-                owner = lax.rem(a + 1 - hc + 2, 2)
+                owner = lax.rem(a + 1 - n // 2 + 2, 2)
                 row = lax.broadcasted_iota(jnp.int32, (512, 128), 0) % 128
                 lane = lax.broadcasted_iota(jnp.int32, (512, 128), 1)
                 lim = row - lane + (y * 256 + owner * 128)
@@ -216,10 +232,12 @@
             run_l[r, :] = run_l[r, :] * jnp.exp2(m - mn) + total
             run_m[r, :] = mn
             mx[zz, r, :] = mn
-            return carry
-
+
+        now = logits(0)
         for n in range(4):
-            tile(n, 0)
+            later = logits(n + 1) if n < 3 else None
+            absorb(n, now)
+            now = later
 
     def hop(i, p):
         p = jnp.int32(p)
@@ -242,16 +260,17 @@
             for d in range(1, NY):
                 y_b(i, p, -1, d).start()
 
-        ring_a(i, p, 1).wait_recv()
-
-        @pl.when(p < 4)
-        def _():
-            ring_a(i, p + 1, 1).start()
-            ring_a(i, p, -1).wait_recv()
-
-        @pl.when(p < 3)
-        def _():
-            ring_a(i, p + 1, -1).start()
+        for e in range(NY):
+            ring_a(i, p, 1, e).wait_recv()
+
+            @pl.when(p < 4)
+            def _():
+                ring_a(i, p + 1, 1, e).start()
+                ring_a(i, p, -1, e).wait_recv()
+
+            @pl.when(p < 3)
+            def _():
+                ring_a(i, p + 1, -1, e).start()
 
     def landed(i, p):
         for d in range(1, NY):
@@ -262,6 +281,19 @@
             for d in range(1, NY):
                 y_b(i, p, -1, d).wait_recv()
 
+    def both_sides(p, work):
+        def side(j, c):
+            up = j == 0
+            zz = jnp.where(up, z - p, z + p - NZ)
+
+            @pl.when((p >= 1) & (zz >= 0) & (up | (p < 4)))
+            def _():
+                work(zz)
+
+            return c
+
+        lax.fori_loop(0, 2, side, 0)
+
     def phase(p, carry):
         @pl.when(p <= 4)
         def _():
@@ -274,6 +306,7 @@
 
         @pl.when(p == 2)
         def _():
+            begin_own(1)
             begin_b(1)
             begin_a(1)
 
@@ -285,20 +318,9 @@
             def _():
                 fold(z, True)
 
-            def side(j, c):
-                up = j == 0
-                zz = jnp.where(up, z - pp, z + pp - NZ)
-                ok = (pp >= 1) & (zz >= 0) & (up | (pp < 4))
-
-                @pl.when(ok)
-                def _():
-                    fold(zz, False)
-
-                return c
-
-            lax.fori_loop(0, 2, side, 0)
-
-        @pl.when(p >= 3)
+            both_sides(pp, lambda zz: fold(zz, False))
+
+        @pl.when((p >= 3) & (p <= 4))
         def _():
             hop(1, p - 2)
 
@@ -311,58 +333,74 @@
 
     def colpass(zz, carry):
         def rows(i, c):
-            r = pl.ds(pl.multiple_of(i * 256, 256), 256)
-            w = jnp.exp2(mx[zz, r, :] - run_m[r, :])
-            mx[zz, r, :] = w
-            out = []
-            for t in range(LANES):
-                x = prob[zz, r, t * 128 : (t + 1) * 128].astype(F32) * w
-                out.append(c[t] + jnp.sum(x.reshape(32, 8, 128), axis=0))
-            return tuple(out)
+            c = list(c)
+            for u in range(32):
+                r = pl.ds(pl.multiple_of(i * 512 + u * 16, 16), 16)
+                w = jnp.exp2(mx[zz, r, :] - run_m[r, :])
+                mx[zz, r, :] = w
+                for t in range(LANES):
+                    x = prob[zz, r, t * 128 : (t + 1) * 128].astype(F32) * w
+                    c[t] = c[t] + x[0:8] + x[8:16]
+            return tuple(c)
 
         c = lax.fori_loop(
-            0, ROWS // 256, rows, tuple(jnp.zeros((8, 128), F32) for _ in range(LANES))
+            0, ROWS // 512, rows, tuple(jnp.zeros((8, 128), F32) for _ in range(LANES))
         )
         for t in range(LANES):
             csum[zz, t : t + 1, :] = jnp.sum(c[t], axis=0, keepdims=True)
         return carry
 
-    half = (z + 1) // 2
-    lax.fori_loop(0, half, colpass, 0)
+    def c1(d):
+        zz = lax.rem(z - d + NZ, NZ)
+        return remote(csum.at[zz], csr.at[d], c1_s.at[d], c1_r.at[d], zoff(-d))
+
+    def columns(k, carry):
+        step = (k + 1) // 2
+        d = jnp.where(lax.rem(k, 2) == 1, 4 - step, 4 + step)
+
+        @pl.when(k == 4)
+        def _():
+            hop(1, 3)
+
+        @pl.when((k == 7) | (d <= z))
+        def _():
+            colpass(jnp.where(k == 7, z, z - d), 0)
+
+        @pl.when(k < 7)
+        def _():
+            c1(d).start()
+
+        return carry
+
+    lax.fori_loop(0, 8, columns, 0)
+
+    acc[...] = jnp.zeros_like(acc)
+    lane = lax.broadcasted_iota(jnp.int32, (8, 128), 1)
+    sub = lax.broadcasted_iota(jnp.int32, (8, 128), 0)
+
+    def weigh(zz):
+        vals = kvb.at[1, zz][...].reshape(SLAB, 128)
+        acc[...] += mx[zz] * jnp.dot(prob[zz], vals, preferred_element_type=F32)
+
+    def weigh_phases(first, last):
+        def one(p, c):
+            landed(1, p)
+
+            @pl.when(p == 0)
+            def _():
+                weigh(z)
+
+            both_sides(p, weigh)
+            return c
+
+        lax.fori_loop(first, last, one, 0)
+
+    weigh_phases(0, 2)
     hop(1, 4)
-    lax.fori_loop(half, z + 1, colpass, 0)
-
-    c1 = [None]
-    for d in range(1, NZ):
-        zz = lax.rem(z - d + NZ, NZ)
-        c1.append(remote(csum.at[zz], csr.at[d], c1_s.at[d], c1_r.at[d], zoff(-d)))
-        c1[d].start()
-
-    lax.fori_loop(0, 5, lambda p, c: (landed(1, p), c)[1], 0)
-
-    def weigh(hc):
-        r = slice(hc * 1024, (hc + 1) * 1024)
-        acc[...] = jnp.zeros_like(acc)
-
-        def one(zz, c):
-            vals = kvb.at[1, zz][...].reshape(SLAB, 128)
-            acc[...] += mx[zz, r, :] * jnp.dot(prob[zz, r, :], vals, preferred_element_type=F32)
-            return c
-
-        lax.fori_loop(0, z + 1, one, 0)
-
-    weigh(0)
-    outs = []
-    for g in range(8):
-        osend[g] = acc[g * 128 : (g + 1) * 128, :].astype(BF16)
-        outs.append(
-            remote(osend.at[g], att_ref.at[:, cols(a * 8 + g)], o_s.at[g], o_r.at[g], sib)
-        )
-        outs[g].start()
 
     total = csum[z]
     for d in range(1, NZ):
-        c1[d].wait_recv()
+        c1(d).wait_recv()
         total = total + csr[d]
     for t in range(8):
         tot8[t] = jnp.broadcast_to(total[t : t + 1, :], (8, 128))
@@ -373,9 +411,7 @@
         )
         c2[d].start()
 
-    weigh(1)
-    for g in range(8):
-        att_ref[:, cols(a * 8 + g)] = acc[g * 128 : (g + 1) * 128, :].astype(BF16)
+    weigh_phases(2, 4)
 
     same = tot8[me8]
     other = jnp.zeros((8, 128), F32)
@@ -385,8 +421,6 @@
             same = same + t2[d]
         else:
             other = other + t2[d]
-    lane = lax.broadcasted_iota(jnp.int32, (8, 128), 1)
-    sub = lax.broadcasted_iota(jnp.int32, (8, 128), 0)
     pos = me * BLK + lane
     factor = (NCTX * BLK / 8.0) / (NCTX * BLK - pos).astype(F32)
     col = [jnp.where(a == 0, same, other) * factor, jnp.where(a == 0, other, same) * factor]
@@ -440,6 +474,17 @@
             row = jnp.sum(jnp.where(lane == sub, scales[n], 0.0), axis=0, keepdims=True)
             scale_ref[0, h, n : n + 1, :] = row[:, 0:8]
 
+    weigh_phases(4, 5)
+    outs = []
+    for g in range(8):
+        osend[g] = acc[g * 128 : (g + 1) * 128, :].astype(BF16)
+        outs.append(
+            remote(osend.at[g], att_ref.at[:, cols(a * 8 + g)], o_s.at[g], o_r.at[g], sib)
+        )
+        outs[g].start()
+    for g in range(8):
+        att_ref[:, cols(a * 8 + g)] = acc[1024 + g * 128 : 1152 + g * 128, :].astype(BF16)
+
     for d in range(1, SPAN):
         sc[d].wait_recv()
     for h in range(2):
@@ -466,11 +511,14 @@
         for p in range(1, 5):
             signs = (1, -1) if p < 4 else (1,)
             for s in signs:
-                ring_a(i, p, s).wait_send()
+                for e in range(NY):
+                    ring_a(i, p, s, e).wait_send()
                 ring_b(i, p, s).wait_send()
                 for d in range(1, NY):
                     y_b(i, p, s, d).wait_send()
-    for group in (pages, c1, c2, im, sc):
+    for d in range(1, NZ):
+        c1(d).wait_send()
+    for group in (pages, c2, im, sc):
         for c in group[1:]:
             c.wait_send()
 
@@ -499,12 +547,13 @@
             pltpu.VMEM((128, 128), F32),
             pltpu.VMEM((128, 128), F32),
             pltpu.VMEM((2, 8, BLK, 128), BF16),
+            pltpu.VMEM((ROWS, 256), BF16),
             pltpu.VMEM((2, NZ, NY, NC, BLK, 128), BF16),
             pltpu.VMEM((NZ, ROWS, SLAB), BF16),
             pltpu.VMEM((NZ, ROWS, 128), F32),
             pltpu.VMEM((ROWS, 128), F32),
             pltpu.VMEM((ROWS, 128), F32),
-            pltpu.VMEM((ROWS // 2, 128), F32),
+            pltpu.VMEM((ROWS, 128), F32),
             pltpu.VMEM((8, BLK, 128), BF16),
             pltpu.VMEM((NZ, 8, 128), F32),
             pltpu.VMEM((NZ, 8, 128), F32),
@@ -520,7 +569,7 @@
             dma((10,)), dma((10,)),
             dma((2, NY)), dma((2, NY)),
             dma((2, 2, 5, NY)), dma((2, 2, 5, NY)),
-            dma((2, 2, 5)), dma((2, 2, 5)),
+            dma((2, 2, 5, NY)), dma((2, 2, 5, NY)),
             dma((2, 2, 5)), dma((2, 2, 5)),
             dma((SPAN,)), dma((SPAN,)),
             dma((NZ,)), dma((NZ,)),

time: 77.9 us -> 73.6 us (0.945)
  Pallas kernels: 77.1 us -> 72.9 us
    pallas_call x1, Pallas kernels: 75.1 us -> 70.9 us  [on_device(): call(queries, key_states, value_states, keep_pages, keep_count, slots)]
where the time goes in v3:
time: 73.6 us; the launch traced here: 73.5 us
  Pallas kernels  72.9 us (99%)
    pallas_call x1, Pallas kernels, on_device(): call(queries, key_states, value_states, keep_pages, keep_count, slots)  70.9 us
    pallas_call x1, Pallas kernels, on_device(): att, imp, tiles, scale, bound, score = hand_over(*made)  1.95 us

profile of v3, /device:TPU:1, one launch (start us, length us, event | category | flops | bytes accessed | tf_op | source)
XLA Modules:
  0.0 73.5 jit_solution(9489737815176581893)
XLA Ops:
  0.6 70.9 %shard_map.109 = (bf16[128,2048]{1,0:T(8,128)(2,1)}, f32[1,128]{1,0:T(1,128)}, bf16[1,2,8,4096]{3,2,1,0:T(8,128)(2,1)}, f32[1,2,2,8]{3,2,1,0:T(2,128)}, f32[1,2,...) custom-call(bf16[128,2048]{1,0:T(8,128)(2,1)} %q_ref.1, bf16[128,256]{1,0:T(8,128)(2,1)} %k_ref.1, bf16[128,256]{1,0:T(8,128)(2,1)} %v_ref.1, ...), custom_call_target="tpu_custom_call" | custom-call | tf_op jit(solution)/shard_map/pallas_call | solution.py:586
  71.6 1.9 %shard_map.110 = (bf16[128,2048]{1,0:T(8,128)(2,1)}, f32[1,128]{1,0:T(1,128)}, bf16[1,2,8,4096]{3,2,1,0:T(8,128)(2,1)}, f32[1,2,2,8]{3,2,1,0:T(2,128)}, f32[1,2,...) custom-call(bf16[128,2048]{1,0:T(8,128)(2,1)} %get-tuple-element.18.refs_0_, f32[1,128]{1,0:T(1,128)} %get-tuple-element.19.refs_1_, ...), custom_call_target="tpu_custom_call" | custom-call | tf_op jit(solution)/shard_map/pallas_call | solution.py:593

commit v4 on v3

--- a/solution.py
+++ b/solution.py
@@ -139,6 +139,8 @@
     for c in local[2:]:
         c.wait()
     begin_a(0)
+    for c in ya[3:]:
+        c.start()
 
     sub8 = lax.broadcasted_iota(jnp.int32, (8, 8), 0)
     lane8 = lax.broadcasted_iota(jnp.int32, (8, 8), 1)
@@ -300,11 +302,6 @@
             hop(0, p)
 
         @pl.when(p == 1)
-        def _():
-            for c in ya[3:]:
-                c.start()
-
-        @pl.when(p == 2)
         def _():
             begin_own(1)
             begin_b(1)

time: 73.6 us -> 75 us (1.019)
  Pallas kernels: 72.9 us -> 74.3 us
    pallas_call x1, Pallas kernels: 70.9 us -> 72.3 us  [on_device(): call(queries, key_states, value_states, keep_pages, keep_count, slots)]
where the time goes in v4:
time: 75 us; the launch traced here: 74.9 us
  Pallas kernels  74.3 us (99%)
    pallas_call x1, Pallas kernels, on_device(): call(queries, key_states, value_states, keep_pages, keep_count, slots)  72.3 us
    pallas_call x1, Pallas kernels, on_device(): att, imp, tiles, scale, bound, score = hand_over(*made)  1.95 us

profile of v4, /device:TPU:1, one launch (start us, length us, event | category | flops | bytes accessed | tf_op | source)
XLA Modules:
  0.0 74.9 jit_solution(2523437045460472632)
XLA Ops:
  0.6 72.3 %shard_map.109 = (bf16[128,2048]{1,0:T(8,128)(2,1)}, f32[1,128]{1,0:T(1,128)}, bf16[1,2,8,4096]{3,2,1,0:T(8,128)(2,1)}, f32[1,2,2,8]{3,2,1,0:T(2,128)}, f32[1,2,...) custom-call(bf16[128,2048]{1,0:T(8,128)(2,1)} %q_ref.1, bf16[128,256]{1,0:T(8,128)(2,1)} %k_ref.1, bf16[128,256]{1,0:T(8,128)(2,1)} %v_ref.1, ...), custom_call_target="tpu_custom_call" | custom-call | tf_op jit(solution)/shard_map/pallas_call | solution.py:583
  73.0 1.9 %shard_map.110 = (bf16[128,2048]{1,0:T(8,128)(2,1)}, f32[1,128]{1,0:T(1,128)}, bf16[1,2,8,4096]{3,2,1,0:T(8,128)(2,1)}, f32[1,2,2,8]{3,2,1,0:T(2,128)}, f32[1,2,...) custom-call(bf16[128,2048]{1,0:T(8,128)(2,1)} %get-tuple-element.18.refs_0_, f32[1,128]{1,0:T(1,128)} %get-tuple-element.19.refs_1_, ...), custom_call_target="tpu_custom_call" | custom-call | tf_op jit(solution)/shard_map/pallas_call | solution.py:590
